TPU v7x, 256 devices: a whole 4x4x8 slice. The times are simulated.
256 devices in a mesh: row: 64 (over y, z, x_hi), col: 4 (over x_lo, core).
Axes of the slice: x: 4 (x_hi: 2, x_lo: 2; x = x_hi * 2 + x_lo), y: 4, z: 8, core: 2. Of those that a mesh axis runs over, the one named last changes fastest.
Arguments:
- table: float32 [128, 1048576], P('col', 'row'), may hold values from -6 to 6
- signs: int32 [1048576], P('row'), may hold values from -1 to 1, as said below
- samples: int32 [8192], replicated, may hold values from 0 to 1048575
Outputs:
- sketch: float32 [128, 8192], P('col', 'row')
- gram: float32 [128, 128], replicated
Inputs may be any that keep to these rules, and one draw needn't show every extreme that they name: `signs`: each entry is 1 or -1.
All inputs are finite; a program needn't handle non-finite values.
Results may differ from a plain program's by a relative error of at most 0.00016.
Values sent between devices are 32-bit elements; how exact they have to be, the bound alone decides.
A program may use at most 64 MiB of HBM per device.

v0:
```python
import math

import jax
import jax.numpy as jnp
from jax import lax
from jax.sharding import PartitionSpec as P

SAMPLES = 8192


def partner_2(block, axis, bit):
    count = lax.axis_size(axis)
    route = []
    for low in range(count):
        high = low | 1 << bit
        if high != low and high < count:
            route += [(low, high), (high, low)]
    return lax.ppermute(block, axis, route)


def walsh_table(order):
    index = lax.iota(jnp.int32, order)
    joined = jnp.bitwise_and(index[:, None], index[None, :])
    parity = jnp.zeros((order, order), jnp.int32)
    for bit_pos in range(max(order.bit_length() - 1, 1)):
        parity = jnp.bitwise_xor(parity, jnp.bitwise_and(jnp.right_shift(joined, bit_pos), 1))
    return (1 - 2 * parity).astype(jnp.float32) / jnp.float32(math.sqrt(order))


def per_device(table, signs, samples):
    width = table.shape[0]
    length = table.shape[1]
    upper_count = length // 128
    signed = table * signs.astype(jnp.float32)[None, :]
    blocks = signed.reshape(width, upper_count, 128)
    blocks = jnp.einsum(
        "cab,ib->cai",
        blocks,
        walsh_table(128),
        precision=lax.Precision.HIGHEST,
        preferred_element_type=jnp.float32,
    )
    blocks = jnp.einsum(
        "cab,ia->cib",
        blocks,
        walsh_table(upper_count),
        precision=lax.Precision.HIGHEST,
        preferred_element_type=jnp.float32,
    )
    mixed = blocks.reshape(width, length)
    devices = lax.axis_size("row")
    position = lax.axis_index("row")
    levels = devices.bit_length() - 1
    factor = jnp.float32(0.7071067811865476)
    order_list = list(range(levels))
    for bit_pos in order_list:
        partner = partner_2(mixed, "row", bit_pos)
        high_side = jnp.bitwise_and(jnp.right_shift(position, bit_pos), 1) == 1
        mixed = jnp.where(high_side, partner - mixed, mixed + partner) * factor
    local_index = samples - position * length
    inside = jnp.logical_and(local_index >= 0, local_index < length)
    chosen = jnp.take(mixed, jnp.clip(local_index, 0, length - 1), axis=1)
    chosen = jnp.where(inside[None, :], chosen, jnp.float32(0.0))
    sketch = lax.psum_scatter(chosen, "row", scatter_dimension=1, tiled=True)
    all_columns = lax.all_gather(sketch, "col", axis=0, tiled=True)
    partial_gram = jnp.dot(
        all_columns,
        all_columns.T,
        precision=lax.Precision.HIGHEST,
        preferred_element_type=jnp.float32,
    )
    gram = lax.psum(partial_gram, "row") / jnp.float32(SAMPLES)
    return (sketch, gram)


def solution(mesh):
    return jax.shard_map(
        per_device,
        mesh=mesh,
        in_specs=(P("col", "row"), P("row"), P()),
        out_specs=(P("col", "row"), P()),
        check_vma=False,
    )
```

profile of v0, /device:TPU:2, one launch (start us, length us, event | category | flops | bytes accessed | tf_op | source)
XLA Modules:
  0.0 1550.4 jit_solution(13113489941317353977)
XLA Ops:
  7.2 0.0 reduce-scatter.2.cloned.1.call-start
  7.2 0.8 convert_element_type.10
  8.1 1.8 multiply_bitcast_fusion
  9.8 0.4 copy.30
  10.2 1.9 fusion.2
  12.2 1.9 fusion
  14.1 1.2 copy.33
  15.3 2.2 collective-permute-start
  17.6 4.6 copy.10
  22.2 42.2 %collective-permute-done = f32[32,16384]{1,0:T(8,128)} collective-permute-done((f32[32,16384]{1,0:T(8,128)S(1)}, f32[32,16384]{1,0:T(8,128)}, u32[]{:S(2)}, u32[]{:S(2)}) %collective-permute-start) | collective-permute-done | bytes 2097184 | tf_op jit(solution)/shard_map/ppermute | solution.py:18
  64.4 6.3 copy.9
  70.7 9.8 select_multiply_fusion.5
  80.5 6.2 copy.13
  86.7 1.9 collective-permute-start.1
  88.6 45.0 %collective-permute-done.1 = f32[32,16384]{1,0:T(8,128)S(1)} collective-permute-done((f32[32,16384]{1,0:T(8,128)}, f32[32,16384]{1,0:T(8,128)S(1)}, u32[]{:S(2)}, u32[]{:S(2)}) %collective-permute-start.1) | collective-permute-done | bytes 2097184 | tf_op jit(solution)/shard_map/ppermute | solution.py:18
  133.6 4.7 copy.14
  138.3 9.8 select_multiply_fusion.4
  148.1 6.2 copy.16
  154.3 3.3 collective-permute-start.2
  157.6 89.2 %collective-permute-done.2 = f32[32,16384]{1,0:T(8,128)S(1)} collective-permute-done((f32[32,16384]{1,0:T(8,128)}, f32[32,16384]{1,0:T(8,128)S(1)}, u32[]{:S(2)}, u32[]{:S(2)}) %collective-permute-start.2) | collective-permute-done | bytes 2097184 | tf_op jit(solution)/shard_map/ppermute | solution.py:18
  246.8 4.7 copy.17
  251.4 9.8 select_multiply_fusion.3
  261.3 6.2 copy.19
  267.5 6.2 collective-permute-start.3
  273.7 91.1 %collective-permute-done.3 = f32[32,16384]{1,0:T(8,128)S(1)} collective-permute-done((f32[32,16384]{1,0:T(8,128)}, f32[32,16384]{1,0:T(8,128)S(1)}, u32[]{:S(2)}, u32[]{:S(2)}) %collective-permute-start.3) | collective-permute-done | bytes 2097184 | tf_op jit(solution)/shard_map/ppermute | solution.py:18
  364.8 4.7 copy.20
  369.4 9.8 select_multiply_fusion.2
  379.3 6.2 copy.22
  385.5 1.6 collective-permute-start.4
  387.1 44.9 %collective-permute-done.4 = f32[32,16384]{1,0:T(8,128)S(1)} collective-permute-done((f32[32,16384]{1,0:T(8,128)}, f32[32,16384]{1,0:T(8,128)S(1)}, u32[]{:S(2)}, u32[]{:S(2)}) %collective-permute-start.4) | collective-permute-done | bytes 2097184 | tf_op jit(solution)/shard_map/ppermute | solution.py:18
  432.1 4.7 copy.23
  436.7 9.8 select_multiply_fusion.1
  446.6 6.2 copy.25
  452.8 3.2 collective-permute-start.5
  456.1 43.9 %collective-permute-done.5 = f32[32,16384]{1,0:T(8,128)S(1)} collective-permute-done((f32[32,16384]{1,0:T(8,128)}, f32[32,16384]{1,0:T(8,128)S(1)}, u32[]{:S(2)}, u32[]{:S(2)}) %collective-permute-start.5) | collective-permute-done | bytes 2097184 | tf_op jit(solution)/shard_map/ppermute | solution.py:18
  500.0 4.7 copy.26
  504.6 9.8 select_multiply_fusion
  514.5 31.1 %gather_fusion = f32[8192,32]{1,0:T(8,128)} fusion(f32[32,16384]{0,1:T(8,128)} %select_multiply_fusion, s32[8192]{0:T(1024)S(1)} %fusion.4), kind=kCustom, calls=%fused_computation | custom fusion | bytes 2129920 | tf_op jit(solution)/shard_map/jit(_take)/gather | solution.py:62
  545.6 7.6 select_bitcast_fusion
  553.2 0.0 reduce-scatter.2.cloned.1.call-update
  553.2 0.0 all-reduce.2.cloned.1.call-start
  553.3 370.4 %reduce-scatter.2.cloned.1.call-done = f32[32,128]{0,1:T(8,128)} async-done(((f32[32,8192]{0,1:T(8,128)}), f32[32,128]{0,1:T(8,128)}) %reduce-scatter.2.cloned.1.call-update) | async-done | bytes 16400 | tf_op jit(solution)/shard_map/reduce_scatter | solution.py:64
  923.6 0.9 copy.29
  924.5 5.3 all_gather.3
  929.8 0.9 fusion.21
  930.7 0.0 all-reduce.2.cloned.1.call-update
  930.7 611.4 %all-reduce.2.cloned.1.call-done = f32[128,128]{1,0:T(8,128)} async-done(((f32[128,128]{1,0:T(8,128)}), f32[128,128]{1,0:T(8,128)}) %all-reduce.2.cloned.1.call-update) | async-done | bytes 65552 | tf_op jit(solution)/shard_map/psum | solution.py:72
  1542.1 1.5 broadcast_multiply_fusion
  (6 shorter events, 0.1 us)
Async XLA Ops:
  7.2 916.5 %reduce-scatter.2.cloned.1.call-start = ((), (), s32[]{:S(2)}) async-start(), calls=%async_computation.1 | async-start | bytes 4259840 | tf_op jit(solution)/shard_map/reduce_scatter | solution.py:64
  15.3 49.1 %collective-permute-start = (f32[32,16384]{1,0:T(8,128)S(1)}, f32[32,16384]{1,0:T(8,128)}, u32[]{:S(2)}, u32[]{:S(2)}) collective-permute-start(f32[32,16384]{1,0:T(8,128)S(1)} %bitcast.19), channel_id=1, source_target_pairs={{0,4},{4,0},{8,12},{12,8},{16,20},{20,16},{24,28},{28,24},{32,36},... | collective-permute-start | bytes 6291464 | tf_op jit(solution)/shard_map/ppermute | solution.py:18
  86.7 46.9 %collective-permute-start.1 = (f32[32,16384]{1,0:T(8,128)}, f32[32,16384]{1,0:T(8,128)S(1)}, u32[]{:S(2)}, u32[]{:S(2)}) collective-permute-start(f32[32,16384]{1,0:T(8,128)} %copy.13), channel_id=1, source_target_pairs={{0,8},{8,0},{4,12},{12,4},{16,24},{24,16},{20,28},{28,20},{32,40},... | collective-permute-start | bytes 6291464 | tf_op jit(solution)/shard_map/ppermute | solution.py:18
  154.3 92.4 %collective-permute-start.2 = (f32[32,16384]{1,0:T(8,128)}, f32[32,16384]{1,0:T(8,128)S(1)}, u32[]{:S(2)}, u32[]{:S(2)}) collective-permute-start(f32[32,16384]{1,0:T(8,128)} %copy.16), channel_id=1, source_target_pairs={{0,16},{16,0},{4,20},{20,4},{8,24},{24,8},{12,28},{28,12},{32,48},... | collective-permute-start | bytes 6291464 | tf_op jit(solution)/shard_map/ppermute | solution.py:18
  267.5 97.3 %collective-permute-start.3 = (f32[32,16384]{1,0:T(8,128)}, f32[32,16384]{1,0:T(8,128)S(1)}, u32[]{:S(2)}, u32[]{:S(2)}) collective-permute-start(f32[32,16384]{1,0:T(8,128)} %copy.19), channel_id=1, source_target_pairs={{0,32},{32,0},{4,36},{36,4},{8,40},{40,8},{12,44},{44,12},{16,48},... | collective-permute-start | bytes 6291464 | tf_op jit(solution)/shard_map/ppermute | solution.py:18
  385.5 46.6 %collective-permute-start.4 = (f32[32,16384]{1,0:T(8,128)}, f32[32,16384]{1,0:T(8,128)S(1)}, u32[]{:S(2)}, u32[]{:S(2)}) collective-permute-start(f32[32,16384]{1,0:T(8,128)} %copy.22), channel_id=1, source_target_pairs={{0,64},{64,0},{4,68},{68,4},{8,72},{72,8},{12,76},{76,12},{16,80},... | collective-permute-start | bytes 6291464 | tf_op jit(solution)/shard_map/ppermute | solution.py:18
  446.6 9.5 copy-start
  452.8 47.2 %collective-permute-start.5 = (f32[32,16384]{1,0:T(8,128)}, f32[32,16384]{1,0:T(8,128)S(1)}, u32[]{:S(2)}, u32[]{:S(2)}) collective-permute-start(f32[32,16384]{1,0:T(8,128)} %copy.25), channel_id=1, source_target_pairs={{0,128},{128,0},{4,132},{132,4},{8,136},{136,8},{12,140},{140,12},... | collective-permute-start | bytes 6291464 | tf_op jit(solution)/shard_map/ppermute | solution.py:18
  553.2 988.9 %all-reduce.2.cloned.1.call-start = ((), (), s32[]{:S(2)}) async-start(), calls=%async_computation.2 | async-start | bytes 131072 | tf_op jit(solution)/shard_map/psum | solution.py:72
  924.5 619.0 %copy-start.1 = (f32[32,128]{1,0:T(8,128)}, f32[32,128]{1,0:T(8,128)S(1)}, u32[]{:S(2)}) copy-start(f32[32,128]{1,0:T(8,128)S(1)} %copy.29) | copy-start | bytes 49156
Sparse Core Ops, SparseCore 0:
  553.4 370.2 reduce-scatter.1
  930.8 611.2 all-reduce.1
where the time goes:
time: 1550 us
  waiting for transfers between devices  1340 us (86%)
  local copies, waits for them, and re-layouts  98.9 us (6%)
  other arithmetic  70.8 us (5%)
  starting transfers between devices  18.6 us (1%)
    psum x1, waiting for transfers between devices, per_device(): gram = lax.psum(partial_gram, 'row') / jnp.float32(SAMPLES)  611 us
    reduce_scatter x1, waiting for transfers between devices, per_device(): sketch = lax.psum_scatter(chosen, 'row', scatter_dimension=1, tiled=True)  370 us
    ppermute x6, waiting for transfers between devices, partner_2(): return lax.ppermute(block, axis, route)  356 us
    mul x6, other arithmetic, per_device(): mixed = jnp.where(high_side, partner - mixed, mixed + partner) * factor  59 us
    mul x5, local copies, waits for them, and re-layouts, per_device(): mixed = jnp.where(high_side, partner - mixed, mixed + partner) * factor  31.2 us
    gather x1, local copies, waits for them, and re-layouts, per_device(): chosen = jnp.take(mixed, jnp.clip(local_index, 0, length - 1), axis=1)  31.1 us
  transfers between devices with their start and end apart: 8, of which 8 were waited for; matrix products, arithmetic and copies ran while one was open for 0% of the time, Pallas kernels for 0%

commit v1 on v0

v1 whole, which is shorter than its diff:
```python
import jax
import jax.numpy as jnp
from jax import lax
from jax.experimental import pallas as pl
from jax.experimental.pallas import tpu as pltpu
from jax.sharding import PartitionSpec as P

F32 = jnp.float32
BF16 = jnp.bfloat16
MESH = pl.DeviceIdType.MESH
NT = (((1,), (1,)), ((), ()))


def butterflies(parts):
    parts = list(parts)
    step = 1
    while step < len(parts):
        for i in range(len(parts)):
            if not i & step:
                a, b = parts[i], parts[i | step]
                parts[i], parts[i | step] = a + b, a - b
        step *= 2
    return parts


def parity(v):
    for shift in (4, 2, 1):
        v = v ^ (v >> shift)
    return v & 1


def split(p):
    a = p.astype(BF16)
    return a, (p - a.astype(F32)).astype(BF16)


def local_kernel(table, signs, samples, out, xs, hi, lo, rows_of, index_v, index_s, sem):
    me = lax.axis_index("row")
    index_v[...] = samples[...] & 16383
    copy = pltpu.make_async_copy(index_v, index_s, sem)
    copy.start()
    for h in range(2):
        rows = slice(16 * h, 16 * h + 16)
        for t in range(2):
            for w in range(8):
                parts = []
                for u in range(8):
                    col = u * 16 + w * 2 + t
                    parts.append(table[rows, col * 128:(col + 1) * 128] * signs[col:col + 1, :].astype(F32))
                for u, p in enumerate(butterflies(parts)):
                    col = u * 16 + w * 2 + t
                    xs[rows, col * 128:(col + 1) * 128] = p
            for u in range(8):
                cols = [u * 16 + w * 2 + t for w in range(8)]
                parts = [xs[rows, col * 128:(col + 1) * 128] for col in cols]
                for w, p in enumerate(butterflies(parts)):
                    a, b = split(p)
                    at = slice(u * 32 + 16 * h, u * 32 + 16 * h + 16)
                    hi[w, at, t * 128:(t + 1) * 128] = a
                    lo[w, at, t * 128:(t + 1) * 128] = b
    i = lax.broadcasted_iota(jnp.int32, (256, 256), 0)
    j = lax.broadcasted_iota(jnp.int32, (256, 256), 1)
    walsh = ((1 - 2 * parity(i & j)).astype(F32) * F32(1 / 1024)).astype(BF16)
    lane = lax.broadcasted_iota(jnp.int32, (256, 128), 1)
    below = [lane < 32, lane < 64, lane < 96]
    for w in range(8):
        done = lax.dot_general(walsh, hi[w], NT, preferred_element_type=F32)
        done = done + lax.dot_general(walsh, lo[w], NT, preferred_element_type=F32)
        for half in range(2):
            tile = done[:, half * 128:half * 128 + 128]
            rolled = [tile] + [pltpu.roll(tile, 32 * k, 1) for k in (1, 2, 3)]
            for x in range(4):
                r = [rolled[(g - x) % 4] for g in range(4)]
                four = jnp.where(below[0], r[0], jnp.where(below[1], r[1], jnp.where(below[2], r[2], r[3])))
                u = half * 4 + x
                rows_of[u * 2048 + w * 256:u * 2048 + w * 256 + 256, :] = four
    copy.wait()
    lane1 = lax.broadcasted_iota(jnp.int32, (1, 128), 1)
    below1 = [lane1 < 32, lane1 < 64, lane1 < 96]

    def chunk(q, carry):
        r = (q // 16) * 16 + (q % 8) * 2 + (q // 8) % 2
        for p in range(32):
            v = [rows_of[pl.ds(index_s[r, g * 32 + p], 1), :] for g in range(4)]
            four = jnp.where(below1[0], v[0], jnp.where(below1[1], v[1], jnp.where(below1[2], v[2], v[3])))
            out[pl.ds(q * 32 + p, 1), :] = four
        return carry

    lax.fori_loop(0, 64, chunk, 0)
    sign = (1 - 2 * parity((samples[...] >> 14) & me)).astype(F32)
    ti = lax.broadcasted_iota(jnp.int32, (32, 128), 1)
    pi = lax.broadcasted_iota(jnp.int32, (32, 128), 0)
    own = (ti & 31) == pi
    bi = lax.broadcasted_iota(jnp.int32, (128, 128), 0)
    bj = lax.broadcasted_iota(jnp.int32, (128, 128), 1)
    spread = ((bi >> 5) == (bj >> 5)).astype(BF16)
    for e in range(8):
        rs = [(e // 2) * 16 + z * 2 + e % 2 for z in range(8)]
        picked = jnp.concatenate([jnp.where(own, sign[r:r + 1, :], F32(0)) for r in rs], axis=0).astype(BF16)
        factor = jnp.dot(picked, spread, preferred_element_type=F32)
        out[e * 256:e * 256 + 256, :] = out[e * 256:e * 256 + 256, :] * factor


def exchange_kernel(terms, sketch, gram, r1, total, r2, whole, r3, r4, blocks, send, recv):
    row = lax.axis_index("row")
    col = lax.axis_index("col")
    y, z, x = row // 16, (row // 2) % 8, row % 2
    e = y * 2 + x

    def plane(k):
        other = (e + k) % 8
        return other, {"row": (other // 2) * 16 + z * 2 + other % 2}

    def line(k):
        other = (z + k) % 8
        return other, {"row": y * 16 + other * 2 + x}

    def column(k):
        return {"col": (col + k) % 4}

    barrier = pltpu.get_barrier_semaphore()
    for k in range(1, 8):
        pl.semaphore_signal(barrier, inc=1, device_id=plane(k)[1], device_id_type=MESH)
        pl.semaphore_signal(barrier, inc=1, device_id=line(k)[1], device_id_type=MESH)
    for k in range(1, 4):
        pl.semaphore_signal(barrier, inc=1, device_id=column(k), device_id_type=MESH)
    pl.semaphore_wait(barrier, 17)

    def start(src, dst, place, device):
        copy = pltpu.make_async_remote_copy(
            src_ref=src, dst_ref=dst, send_sem=send.at[place], recv_sem=recv.at[place], device_id=device, device_id_type=MESH
        )
        copy.start()
        return copy

    started = []

    def landed(copies):
        for copy in copies:
            copy.wait_recv()
        started.extend(copies)

    copies = []
    for k in range(1, 8):
        other, device = plane(k)
        copies.append(start(terms.at[pl.ds(other * 256, 256)], r1.at[k - 1], k - 1, device))
    landed(copies)
    acc = terms[pl.ds(pl.multiple_of(e * 256, 256), 256), :]
    for k in range(7):
        acc = acc + r1[k]
    total[...] = acc
    copies = []
    for k in range(1, 8):
        other, device = line(k)
        copies.append(start(total.at[pl.ds(other * 32, 32)], r2.at[k - 1], 7 + k - 1, device))
    landed(copies)
    acc = total[pl.ds(pl.multiple_of(z * 32, 32), 32), :]
    for k in range(7):
        acc = acc + r2[k]
    mine = jnp.concatenate([acc[:, g * 32:g * 32 + 32].T for g in range(4)], axis=1)
    sketch[...] = mine
    whole[col] = mine
    landed([start(whole.at[col], whole.at[col], 14 + k - 1, column(k)) for k in range(1, 4)])
    every = whole[...].reshape(128, 128)
    part = lax.dot_general(mine, every, NT, precision=lax.Precision.HIGHEST, preferred_element_type=F32)
    r3[e] = part
    landed([start(r3.at[e], r3.at[e], 17 + k - 1, plane(k)[1]) for k in range(1, 8)])
    acc = r3[0]
    for k in range(1, 8):
        acc = acc + r3[k]
    r4[z] = acc
    landed([start(r4.at[z], r4.at[z], 24 + k - 1, line(k)[1]) for k in range(1, 8)])
    acc = r4[0]
    for k in range(1, 8):
        acc = acc + r4[k]
    blocks[col] = acc * F32(1 / 8192)
    landed([start(blocks.at[col], blocks.at[col], 31 + k - 1, column(k)) for k in range(1, 4)])
    gram[...] = blocks[...].reshape(128, 128)
    for copy in started:
        copy.wait_send()


def per_device(table, signs, samples):
    vmem = pl.BlockSpec(memory_space=pltpu.VMEM)
    terms = pl.pallas_call(
        local_kernel,
        out_shape=jax.ShapeDtypeStruct((2048, 128), F32),
        in_specs=[vmem] * 3,
        out_specs=vmem,
        scratch_shapes=[
            pltpu.VMEM((32, 16384), F32),
            pltpu.VMEM((8, 256, 256), BF16),
            pltpu.VMEM((8, 256, 256), BF16),
            pltpu.VMEM((16384, 128), F32),
            pltpu.VMEM((64, 128), jnp.int32),
            pltpu.SMEM((64, 128), jnp.int32),
            pltpu.SemaphoreType.DMA,
        ],
        compiler_params=pltpu.CompilerParams(vmem_limit_bytes=40 * 2**20),
    )(table, signs.reshape(128, 128), samples.reshape(64, 128))
    return pl.pallas_call(
        exchange_kernel,
        out_shape=(jax.ShapeDtypeStruct((32, 128), F32), jax.ShapeDtypeStruct((128, 128), F32)),
        in_specs=[vmem],
        out_specs=(vmem, vmem),
        scratch_shapes=[
            pltpu.VMEM((7, 256, 128), F32),
            pltpu.VMEM((256, 128), F32),
            pltpu.VMEM((7, 32, 128), F32),
            pltpu.VMEM((4, 32, 128), F32),
            pltpu.VMEM((8, 32, 128), F32),
            pltpu.VMEM((8, 32, 128), F32),
            pltpu.VMEM((4, 32, 128), F32),
            pltpu.SemaphoreType.DMA((34,)),
            pltpu.SemaphoreType.DMA((34,)),
        ],
        compiler_params=pltpu.CompilerParams(
            collective_id=0, has_side_effects=True, vmem_limit_bytes=24 * 2**20
        ),
    )(terms)


def solution(mesh):
    return jax.shard_map(
        per_device,
        mesh=mesh,
        in_specs=(P("col", "row"), P("row"), P()),
        out_specs=(P("col", "row"), P()),
        check_vma=False,
    )
```

time: 1550 us -> 64.1 us (0.04)
  the two profiles are of different devices: /device:TPU:2 before, /device:TPU:1 now
where the time goes in v1:
time: 64.1 us; the launch traced here: 63.9 us
  Pallas kernels  58.8 us (92%)
  local copies, waits for them, and re-layouts  4.42 us (7%)
  between operations  0.66 us (1%)
    pallas_call x1, Pallas kernels, per_device(): pl.pallas_call(exchange_kernel, out_shape=(jax.ShapeDtypeStruct((32, 128)...  46.7 us
    pallas_call x1, Pallas kernels, per_device(): pl.pallas_call(local_kernel, out_shape=jax.ShapeDtypeStruct((2048, 128),...  12 us
    unnamed x8, local copies, waits for them, and re-layouts  4.42 us

profile of v1, /device:TPU:1, one launch (start us, length us, event | category | flops | bytes accessed | tf_op | source)
XLA Modules:
  0.0 63.9 jit_solution(2946670365148830299)
XLA Ops:
  0.6 0.0 copy-start
  0.6 1.6 %copy-done = f32[32,16384]{1,0:T(8,128)S(1)} copy-done((f32[32,16384]{1,0:T(8,128)S(1)}, f32[32,16384]{1,0:T(8,128)}, u32[]{:S(2)}) %copy-start) | copy-done | bytes 2097176
  2.2 0.0 copy-start.1
  2.2 0.8 %copy-done.1 = s32[16384]{0:T(1024)S(1)} copy-done((s32[16384]{0:T(1024)S(1)}, s32[16384]{0:T(1024)}, u32[]{:S(2)}) %copy-start.1) | copy-done | bytes 65560
  3.1 0.0 copy-start.2
  3.1 0.8 %copy-done.2 = s32[8192]{0:T(1024)S(1)} copy-done((s32[8192]{0:T(1024)S(1)}, s32[8192]{0:T(1024)}, u32[]{:S(2)}) %copy-start.2) | copy-done | bytes 32792
  3.8 12.0 %shard_map.50.terms = f32[2048,128]{1,0:T(8,128)S(1)} custom-call(f32[32,16384]{1,0:T(8,128)S(1)} %copy-done, s32[128,128]{1,0:T(8,128)S(1)} %bitcast.2, s32[64,128]{1,0:T(8,128)S(1)} %bitcast.3), custom_call_target="tpu_custom_call" | custom-call | tf_op jit(solution)/shard_map/pallas_call | solution.py:185
  15.9 46.7 %shard_map.51 = (f32[32,128]{1,0:T(8,128)S(1)}, f32[128,128]{1,0:T(8,128)S(1)}) custom-call(f32[2048,128]{1,0:T(8,128)S(1)} %shard_map.50.terms), custom_call_target="tpu_custom_call" | custom-call | tf_op jit(solution)/shard_map/pallas_call | solution.py:201
  62.6 0.6 copy.7
  63.2 0.6 copy.8
Async XLA Ops:
  0.6 1.6 %copy-start = (f32[32,16384]{1,0:T(8,128)S(1)}, f32[32,16384]{1,0:T(8,128)}, u32[]{:S(2)}) copy-start(f32[32,16384]{1,0:T(8,128)} %table.1) | copy-start | bytes 6291460
  2.2 0.8 %copy-start.1 = (s32[16384]{0:T(1024)S(1)}, s32[16384]{0:T(1024)}, u32[]{:S(2)}) copy-start(s32[16384]{0:T(1024)} %param.4) | copy-start | bytes 196612
  3.1 0.8 %copy-start.2 = (s32[8192]{0:T(1024)S(1)}, s32[8192]{0:T(1024)}, u32[]{:S(2)}) copy-start(s32[8192]{0:T(1024)} %param.5) | copy-start | bytes 98308

commit v2 on v1

v2 whole, which is shorter than its diff:
```python
import jax
import jax.numpy as jnp
from jax import lax
from jax.experimental import pallas as pl
from jax.experimental.pallas import tpu as pltpu
from jax.sharding import PartitionSpec as P

F32 = jnp.float32
BF16 = jnp.bfloat16
MESH = pl.DeviceIdType.MESH
NT = (((1,), (1,)), ((), ()))


def butterflies(parts):
    parts = list(parts)
    step = 1
    while step < len(parts):
        for i in range(len(parts)):
            if not i & step:
                a, b = parts[i], parts[i | step]
                parts[i], parts[i | step] = a + b, a - b
        step *= 2
    return parts


def parity(v):
    for shift in (4, 2, 1):
        v = v ^ (v >> shift)
    return v & 1


def split(p):
    a = p.astype(BF16)
    return a, (p - a.astype(F32)).astype(BF16)


def kernel(
    table_hbm, signs_hbm, samples_hbm, sketch, gram,
    table, signs, samples, xs, hi, lo, rows_of, index_v, index_s, sign_of, terms, r1, total, r2, whole, r3, r4, blocks,
    load, send, recv,
):
    row = lax.axis_index("row")
    col = lax.axis_index("col")
    y, z, x = row // 16, (row // 2) % 8, row % 2
    line_place = x * 4 + col

    def plane(dy, dx):
        return (y + dy) % 4, (x + dx) % 2

    def at(y, z, x):
        return {"row": y * 16 + z * 2 + x}

    def x_line(k):
        other = (line_place + k) % 8
        return {"row": y * 16 + z * 2 + other // 4, "col": other % 4}

    partners = [(2, 1), (1, 1), (3, 1), (2, 0), (0, 1), (1, 0), (3, 0)]
    copies_in = [
        pltpu.make_async_copy(signs_hbm, signs, load.at[0]),
        pltpu.make_async_copy(table_hbm.at[pl.ds(0, 16)], table.at[pl.ds(0, 16)], load.at[1]),
        pltpu.make_async_copy(samples_hbm, samples, load.at[2]),
        pltpu.make_async_copy(table_hbm.at[pl.ds(16, 16)], table.at[pl.ds(16, 16)], load.at[3]),
    ]
    for copy in copies_in:
        copy.start()
    barrier = pltpu.get_barrier_semaphore()
    met = [at(*(lambda o: (o[0], z, o[1]))(plane(dy, dx))) for dy, dx in partners]
    met += [at(y, (z + k) % 8, x) for k in range(1, 8)]
    met += [{"row": y * 16 + z * 2 + (x + dx) % 2, "col": (col + dc) % 4} for dx in range(2) for dc in range(1, 4)]
    for device in met:
        pl.semaphore_signal(barrier, inc=1, device_id=device, device_id_type=MESH)

    i = lax.broadcasted_iota(jnp.int32, (256, 256), 0)
    j = lax.broadcasted_iota(jnp.int32, (256, 256), 1)
    walsh = ((1 - 2 * parity(i & j)).astype(F32) * F32(1 / 1024)).astype(BF16)
    copies_in[0].wait()
    for h in range(2):
        rows = slice(16 * h, 16 * h + 16)
        copies_in[1 + 2 * h].wait()
        for t in range(2):
            for w in range(8):
                parts = []
                for u in range(8):
                    c = u * 16 + w * 2 + t
                    parts.append(table[rows, c * 128:(c + 1) * 128] * signs[c:c + 1, :].astype(F32))
                for u, p in enumerate(butterflies(parts)):
                    c = u * 16 + w * 2 + t
                    xs[rows, c * 128:(c + 1) * 128] = p
            for u in range(8):
                cs = [u * 16 + w * 2 + t for w in range(8)]
                parts = [xs[rows, c * 128:(c + 1) * 128] for c in cs]
                for w, p in enumerate(butterflies(parts)):
                    a, b = split(p)
                    put = slice(u * 32 + 16 * h, u * 32 + 16 * h + 16)
                    hi[w, put, t * 128:(t + 1) * 128] = a
                    lo[w, put, t * 128:(t + 1) * 128] = b
        if h == 0:
            copies_in[2].wait()
            index_v[...] = samples[...] & 16383
            index_copy = pltpu.make_async_copy(index_v, index_s, load.at[4])
            index_copy.start()
            sign_of[...] = (1 - 2 * parity((samples[...] >> 14) & row)).astype(F32)
    lane = lax.broadcasted_iota(jnp.int32, (256, 128), 1)
    below = [lane < 32, lane < 64, lane < 96]
    for w in range(8):
        done = lax.dot_general(walsh, hi[w], NT, preferred_element_type=F32)
        done = done + lax.dot_general(walsh, lo[w], NT, preferred_element_type=F32)
        for half in range(2):
            tile = done[:, half * 128:half * 128 + 128]
            rolled = [tile] + [pltpu.roll(tile, 32 * k, 1) for k in (1, 2, 3)]
            for v in range(4):
                r = [rolled[(g - v) % 4] for g in range(4)]
                four = jnp.where(below[0], r[0], jnp.where(below[1], r[1], jnp.where(below[2], r[2], r[3])))
                u = half * 4 + v
                rows_of[u * 2048 + w * 256:u * 2048 + w * 256 + 256, :] = four
    index_copy.wait()
    pl.semaphore_wait(barrier, len(met))

    lane1 = lax.broadcasted_iota(jnp.int32, (1, 128), 1)
    below1 = [lane1 < 32, lane1 < 64, lane1 < 96]
    own = (lax.broadcasted_iota(jnp.int32, (32, 128), 1) & 31) == lax.broadcasted_iota(jnp.int32, (32, 128), 0)
    spread = (
        (lax.broadcasted_iota(jnp.int32, (128, 128), 0) >> 5) == (lax.broadcasted_iota(jnp.int32, (128, 128), 1) >> 5)
    ).astype(BF16)

    def gather(slot, y_of, x_of):
        def chunk(q, carry):
            r = y_of * 16 + q * 2 + x_of
            base = slot * 256 + q * 32
            picked = jnp.where(own, sign_of[pl.ds(r, 1), :], F32(0)).astype(BF16)
            factor = jnp.dot(picked, spread, preferred_element_type=F32)
            for p in range(32):
                v = [rows_of[pl.ds(index_s[r, g * 32 + p], 1), :] for g in range(4)]
                four = jnp.where(below1[0], v[0], jnp.where(below1[1], v[1], jnp.where(below1[2], v[2], v[3])))
                terms[pl.ds(base + p, 1), :] = four
            here = pl.ds(pl.multiple_of(base, 32), 32)
            terms[here, :] = terms[here, :] * factor
            return carry

        lax.fori_loop(0, 8, chunk, 0)

    def start(src, dst, place, device):
        copy = pltpu.make_async_remote_copy(
            src_ref=src, dst_ref=dst, send_sem=send.at[place], recv_sem=recv.at[place], device_id=device, device_id_type=MESH
        )
        copy.start()
        return copy

    started = []

    def landed(copies):
        for copy in copies:
            copy.wait_recv()
        started.extend(copies)

    copies = []
    for k, (dy, dx) in enumerate(partners):
        y_of, x_of = plane(dy, dx)
        gather(k, y_of, x_of)
        copies.append(start(terms.at[pl.ds(k * 256, 256)], r1.at[k], k, at(y_of, z, x_of)))
    gather(7, y, x)
    landed(copies)
    acc = terms[7 * 256:8 * 256, :]
    for k in range(7):
        acc = acc + r1[k]
    total[...] = acc
    copies = []
    for k in (4, 3, 5, 2, 6, 1, 7):
        other = (z + k) % 8
        copies.append(start(total.at[pl.ds(other * 32, 32)], r2.at[k - 1], 7 + k - 1, at(y, other, x)))
    landed(copies)
    acc = total[pl.ds(pl.multiple_of(z * 32, 32), 32), :]
    for k in range(7):
        acc = acc + r2[k]
    mine = jnp.concatenate([acc[:, g * 32:g * 32 + 32].T for g in range(4)], axis=1)
    sketch[...] = mine
    whole[line_place] = mine
    landed([start(whole.at[line_place], whole.at[line_place], 14 + k - 1, x_line(k)) for k in range(1, 8)])
    part = jnp.zeros((16, 128), F32)
    for half in range(2):
        every = jnp.concatenate([whole[half * 4 + c] for c in range(4)], axis=0)
        left = whole[half * 4 + line_place // 2, pl.ds(pl.multiple_of((line_place % 2) * 16, 16), 16), :]
        part = part + lax.dot_general(left, every, NT, precision=lax.Precision.HIGHEST, preferred_element_type=F32)
    r3[y] = part
    landed([start(r3.at[y], r3.at[y], 21 + k - 1, at((y + k) % 4, z, x)) for k in (2, 1, 3)])
    acc = (r3[0] + r3[1]) + (r3[2] + r3[3])
    r4[z] = acc
    landed([start(r4.at[z], r4.at[z], 24 + k - 1, at(y, (z + k) % 8, x)) for k in (4, 3, 5, 2, 6, 1, 7)])
    acc = ((r4[0] + r4[1]) + (r4[2] + r4[3])) + ((r4[4] + r4[5]) + (r4[6] + r4[7]))
    blocks[line_place] = acc * F32(1 / 8192)
    landed([start(blocks.at[line_place], blocks.at[line_place], 31 + k - 1, x_line(k)) for k in range(1, 8)])
    gram[...] = blocks[...].reshape(128, 128)
    for copy in started:
        copy.wait_send()


def per_device(table, signs, samples):
    hbm = pl.BlockSpec(memory_space=pltpu.HBM)
    vmem = pl.BlockSpec(memory_space=pltpu.VMEM)
    return pl.pallas_call(
        kernel,
        out_shape=(jax.ShapeDtypeStruct((32, 128), F32), jax.ShapeDtypeStruct((128, 128), F32)),
        in_specs=[hbm] * 3,
        out_specs=(vmem, vmem),
        scratch_shapes=[
            pltpu.VMEM((32, 16384), F32),
            pltpu.VMEM((128, 128), jnp.int32),
            pltpu.VMEM((64, 128), jnp.int32),
            pltpu.VMEM((32, 16384), F32),
            pltpu.VMEM((8, 256, 256), BF16),
            pltpu.VMEM((8, 256, 256), BF16),
            pltpu.VMEM((16384, 128), F32),
            pltpu.VMEM((64, 128), jnp.int32),
            pltpu.SMEM((64, 128), jnp.int32),
            pltpu.VMEM((64, 128), F32),
            pltpu.VMEM((2048, 128), F32),
            pltpu.VMEM((7, 256, 128), F32),
            pltpu.VMEM((256, 128), F32),
            pltpu.VMEM((7, 32, 128), F32),
            pltpu.VMEM((8, 32, 128), F32),
            pltpu.VMEM((4, 16, 128), F32),
            pltpu.VMEM((8, 16, 128), F32),
            pltpu.VMEM((8, 16, 128), F32),
            pltpu.SemaphoreType.DMA((5,)),
            pltpu.SemaphoreType.DMA((38,)),
            pltpu.SemaphoreType.DMA((38,)),
        ],
        compiler_params=pltpu.CompilerParams(collective_id=0, has_side_effects=True, vmem_limit_bytes=40 * 2**20),
    )(table, signs.reshape(128, 128), samples.reshape(64, 128))


def solution(mesh):
    return jax.shard_map(
        per_device,
        mesh=mesh,
        in_specs=(P("col", "row"), P("row"), P()),
        out_specs=(P("col", "row"), P()),
        check_vma=False,
    )
```

time: 64.1 us -> 54.5 us (0.85)
  Pallas kernels: 58.8 us -> 49.2 us
    pallas_call x2 -> x1, Pallas kernels: 58.8 us -> 49.2 us  [per_device(): pl.pallas_call(kernel, out_shape=(jax.ShapeDtypeStruct((32, 128), F32), j...]
where the time goes in v2:
time: 54.5 us; the launch traced here: 54.2 us
  Pallas kernels  49.2 us (90%)
  local copies, waits for them, and re-layouts  4.42 us (8%)
  between operations  0.65 us (1%)
    pallas_call x1, Pallas kernels, per_device(): pl.pallas_call(kernel, out_shape=(jax.ShapeDtypeStruct((32, 128), F32), j...  49.2 us
    unnamed x8, local copies, waits for them, and re-layouts  4.42 us

profile of v2, /device:TPU:1, one launch (start us, length us, event | category | flops | bytes accessed | tf_op | source)
XLA Modules:
  0.0 54.2 jit_solution(1906680996844230211)
XLA Ops:
  0.6 0.0 copy-start
  0.6 1.6 %copy-done = f32[32,16384]{1,0:T(8,128)S(1)} copy-done((f32[32,16384]{1,0:T(8,128)S(1)}, f32[32,16384]{1,0:T(8,128)}, u32[]{:S(2)}) %copy-start) | copy-done | bytes 2097176
  2.2 0.0 copy-start.1
  2.2 0.8 %copy-done.1 = s32[16384]{0:T(1024)S(1)} copy-done((s32[16384]{0:T(1024)S(1)}, s32[16384]{0:T(1024)}, u32[]{:S(2)}) %copy-start.1) | copy-done | bytes 65560
  3.1 0.0 copy-start.2
  3.1 0.8 %copy-done.2 = s32[8192]{0:T(1024)S(1)} copy-done((s32[8192]{0:T(1024)S(1)}, s32[8192]{0:T(1024)}, u32[]{:S(2)}) %copy-start.2) | copy-done | bytes 32792
  3.8 49.2 %shard_map.50 = (f32[32,128]{1,0:T(8,128)S(1)}, f32[128,128]{1,0:T(8,128)S(1)}) custom-call(f32[32,16384]{1,0:T(8,128)S(1)} %copy-done, s32[128,128]{1,0:T(8,128)S(1)} %bitcast.2, s32[64,128]{1,0:T(8,128)S(1)} %bitcast.3), custom_call_target="tpu_custom_call" | custom-call | tf_op jit(solution)/shard_map/pallas_call | solution.py:200
  53.0 0.6 %copy.7 = f32[32,128]{1,0:T(8,128)} copy(f32[32,128]{1,0:T(8,128)S(1)} %get-tuple-element.4) | data formatting | bytes 32768
  53.6 0.6 %copy.8 = f32[128,128]{1,0:T(8,128)} copy(f32[128,128]{1,0:T(8,128)S(1)} %get-tuple-element.5) | data formatting | bytes 131072
Async XLA Ops:
  0.6 1.6 %copy-start = (f32[32,16384]{1,0:T(8,128)S(1)}, f32[32,16384]{1,0:T(8,128)}, u32[]{:S(2)}) copy-start(f32[32,16384]{1,0:T(8,128)} %table_hbm.1) | copy-start | bytes 6291460
  2.2 0.8 %copy-start.1 = (s32[16384]{0:T(1024)S(1)}, s32[16384]{0:T(1024)}, u32[]{:S(2)}) copy-start(s32[16384]{0:T(1024)} %param.4) | copy-start | bytes 196612
  3.1 0.8 %copy-start.2 = (s32[8192]{0:T(1024)S(1)}, s32[8192]{0:T(1024)}, u32[]{:S(2)}) copy-start(s32[8192]{0:T(1024)} %param.5) | copy-start | bytes 98308

commit v3 on v2

--- a/solution.py
+++ b/solution.py
@@ -36,7 +36,8 @@
 
 def kernel(
     table_hbm, signs_hbm, samples_hbm, sketch, gram,
-    table, signs, samples, xs, hi, lo, rows_of, index_v, index_s, sign_of, terms, r1, total, r2, whole, r3, r4, blocks,
+    table, signs, samples, xs, hi, lo, rows_of, index_v, index_s, sign_of, terms_z, z1, total_z, z2, terms, r1, total, r2,
+    whole, r3, r4, blocks,
     load, send, recv,
 ):
     row = lax.axis_index("row")
@@ -118,33 +119,62 @@
 
     lane1 = lax.broadcasted_iota(jnp.int32, (1, 128), 1)
     below1 = [lane1 < 32, lane1 < 64, lane1 < 96]
-    own = (lax.broadcasted_iota(jnp.int32, (32, 128), 1) & 31) == lax.broadcasted_iota(jnp.int32, (32, 128), 0)
     spread = (
         (lax.broadcasted_iota(jnp.int32, (128, 128), 0) >> 5) == (lax.broadcasted_iota(jnp.int32, (128, 128), 1) >> 5)
     ).astype(BF16)
 
-    def gather(slot, y_of, x_of):
-        def chunk(q, carry):
-            r = y_of * 16 + q * 2 + x_of
-            base = slot * 256 + q * 32
-            picked = jnp.where(own, sign_of[pl.ds(r, 1), :], F32(0)).astype(BF16)
-            factor = jnp.dot(picked, spread, preferred_element_type=F32)
-            for p in range(32):
-                v = [rows_of[pl.ds(index_s[r, g * 32 + p], 1), :] for g in range(4)]
+    def own(first, count):
+        shape = (count, 128)
+        return (lax.broadcasted_iota(jnp.int32, shape, 1) & 31) == lax.broadcasted_iota(jnp.int32, shape, 0) + first
+
+    def gather(into, to, first, count, rs):
+        mask = own(first, count)
+        picked = [jnp.where(mask, sign_of[pl.ds(r, 1), :], F32(0)) for r in rs]
+        factor = jnp.dot(jnp.concatenate(picked, axis=0).astype(BF16), spread, preferred_element_type=F32)
+        for n, r in enumerate(rs):
+            for p in range(count):
+                v = [rows_of[pl.ds(index_s[r, g * 32 + first + p], 1), :] for g in range(4)]
                 four = jnp.where(below1[0], v[0], jnp.where(below1[1], v[1], jnp.where(below1[2], v[2], v[3])))
-                terms[pl.ds(base + p, 1), :] = four
-            here = pl.ds(pl.multiple_of(base, 32), 32)
-            terms[here, :] = terms[here, :] * factor
+                into[pl.ds(to + n * count + p, 1), :] = four
+        here = pl.ds(pl.multiple_of(to, 8), len(rs) * count)
+        into[here, :] = into[here, :] * factor
+
+    def gather_z(n):
+        _, other = line(n)
+
+        def four(q, carry):
+            gather(terms_z, n * 64 + q * 32, 0, 8, [(2 * q + e // 2) * 16 + other * 2 + e % 2 for e in range(4)])
             return carry
 
-        lax.fori_loop(0, 8, chunk, 0)
-
-    def start(src, dst, place, device):
-        copy = pltpu.make_async_remote_copy(
+        lax.fori_loop(0, 2, four, 0)
+
+    def gather_yx(n, s):
+        y_of, x_of = turned(n)
+        gather(terms, n * 192 + s * 48, 8, 24, [y_of * 16 + (2 * s + j) * 2 + x_of for j in range(2)])
+
+    def line(n):
+        k = jnp.where(n == 7, 0, (n + 4) % 8 + n // 4)
+        return k, (z + k) % 8
+
+    def turned(n):
+        return (y + (7 - n) // 2) % 4, (x + (7 - n) % 2) % 2
+
+    def remote(src, dst, place, device):
+        return pltpu.make_async_remote_copy(
             src_ref=src, dst_ref=dst, send_sem=send.at[place], recv_sem=recv.at[place], device_id=device, device_id_type=MESH
         )
+
+    def start(src, dst, place, device):
+        copy = remote(src, dst, place, device)
         copy.start()
         return copy
+
+    def sent_z(n):
+        return remote(terms_z.at[pl.ds(n * 64, 64)], z1.at[n], n, at(y, line(n)[1], x))
+
+    def sent_yx(n, s):
+        y_of, x_of = turned(n)
+        return remote(terms.at[pl.ds(n * 192 + s * 48, 48)], r1.at[n, pl.ds(s * 48, 48)], 7 + n * 4 + s, at(y_of, z, x_of))
 
     started = []
 
@@ -153,42 +183,68 @@
             copy.wait_recv()
         started.extend(copies)
 
+    def added(own_part, slots):
+        acc = own_part
+        for k in range(7):
+            acc = acc + slots[k]
+        return acc
+
+    def step(s, carry):
+        def of_z(n, carry):
+            gather_z(n)
+            sent_z(n).start()
+            return carry
+
+        def of_yx(n, carry):
+            gather_yx(n, s)
+            sent_yx(n, s).start()
+            return carry
+
+        lax.fori_loop(2 * s, jnp.minimum(2 * s + 2, 7), of_z, 0)
+        lax.fori_loop(0, 7, of_yx, 0)
+        return carry
+
+    lax.fori_loop(0, 4, step, 0)
+    gather_z(7)
+
+    def of_own(s, carry):
+        gather_yx(7, s)
+        return carry
+
+    lax.fori_loop(0, 4, of_own, 0)
+    landed([sent_z(n) for n in range(7)])
+    total_z[...] = added(terms_z[7 * 64:8 * 64, :], z1)
+    copies_z = []
+    for n in range(7):
+        y_of, x_of = turned(n)
+        copies_z.append(start(total_z.at[pl.ds((y_of * 2 + x_of) * 8, 8)], z2.at[n], 35 + n, at(y_of, z, x_of)))
+    landed([sent_yx(n, s) for s in range(4) for n in range(7)])
+    total[...] = added(terms[7 * 192:8 * 192, :], r1)
     copies = []
-    for k, (dy, dx) in enumerate(partners):
-        y_of, x_of = plane(dy, dx)
-        gather(k, y_of, x_of)
-        copies.append(start(terms.at[pl.ds(k * 256, 256)], r1.at[k], k, at(y_of, z, x_of)))
-    gather(7, y, x)
+    for n in range(7):
+        other = line(n)[1]
+        copies.append(start(total.at[pl.ds(other * 24, 24)], r2.at[n], 42 + n, at(y, other, x)))
+    landed(copies_z)
+    acc_z = added(total_z[pl.ds(pl.multiple_of((y * 2 + x) * 8, 8), 8), :], z2)
     landed(copies)
-    acc = terms[7 * 256:8 * 256, :]
-    for k in range(7):
-        acc = acc + r1[k]
-    total[...] = acc
-    copies = []
-    for k in (4, 3, 5, 2, 6, 1, 7):
-        other = (z + k) % 8
-        copies.append(start(total.at[pl.ds(other * 32, 32)], r2.at[k - 1], 7 + k - 1, at(y, other, x)))
-    landed(copies)
-    acc = total[pl.ds(pl.multiple_of(z * 32, 32), 32), :]
-    for k in range(7):
-        acc = acc + r2[k]
+    acc = jnp.concatenate([acc_z, added(total[pl.ds(pl.multiple_of(z * 24, 8), 24), :], r2)], axis=0)
     mine = jnp.concatenate([acc[:, g * 32:g * 32 + 32].T for g in range(4)], axis=1)
     sketch[...] = mine
     whole[line_place] = mine
-    landed([start(whole.at[line_place], whole.at[line_place], 14 + k - 1, x_line(k)) for k in range(1, 8)])
+    landed([start(whole.at[line_place], whole.at[line_place], 49 + k - 1, x_line(k)) for k in range(1, 8)])
     part = jnp.zeros((16, 128), F32)
     for half in range(2):
         every = jnp.concatenate([whole[half * 4 + c] for c in range(4)], axis=0)
         left = whole[half * 4 + line_place // 2, pl.ds(pl.multiple_of((line_place % 2) * 16, 16), 16), :]
         part = part + lax.dot_general(left, every, NT, precision=lax.Precision.HIGHEST, preferred_element_type=F32)
     r3[y] = part
-    landed([start(r3.at[y], r3.at[y], 21 + k - 1, at((y + k) % 4, z, x)) for k in (2, 1, 3)])
+    landed([start(r3.at[y], r3.at[y], 56 + k - 1, at((y + k) % 4, z, x)) for k in (2, 1, 3)])
     acc = (r3[0] + r3[1]) + (r3[2] + r3[3])
     r4[z] = acc
-    landed([start(r4.at[z], r4.at[z], 24 + k - 1, at(y, (z + k) % 8, x)) for k in (4, 3, 5, 2, 6, 1, 7)])
+    landed([start(r4.at[z], r4.at[z], 59 + k - 1, at(y, (z + k) % 8, x)) for k in (4, 3, 5, 2, 6, 1, 7)])
     acc = ((r4[0] + r4[1]) + (r4[2] + r4[3])) + ((r4[4] + r4[5]) + (r4[6] + r4[7]))
     blocks[line_place] = acc * F32(1 / 8192)
-    landed([start(blocks.at[line_place], blocks.at[line_place], 31 + k - 1, x_line(k)) for k in range(1, 8)])
+    landed([start(blocks.at[line_place], blocks.at[line_place], 66 + k - 1, x_line(k)) for k in range(1, 8)])
     gram[...] = blocks[...].reshape(128, 128)
     for copy in started:
         copy.wait_send()
@@ -213,19 +269,23 @@
             pltpu.VMEM((64, 128), jnp.int32),
             pltpu.SMEM((64, 128), jnp.int32),
             pltpu.VMEM((64, 128), F32),
-            pltpu.VMEM((2048, 128), F32),
-            pltpu.VMEM((7, 256, 128), F32),
-            pltpu.VMEM((256, 128), F32),
-            pltpu.VMEM((7, 32, 128), F32),
+            pltpu.VMEM((512, 128), F32),
+            pltpu.VMEM((7, 64, 128), F32),
+            pltpu.VMEM((64, 128), F32),
+            pltpu.VMEM((7, 8, 128), F32),
+            pltpu.VMEM((1536, 128), F32),
+            pltpu.VMEM((7, 192, 128), F32),
+            pltpu.VMEM((192, 128), F32),
+            pltpu.VMEM((7, 24, 128), F32),
             pltpu.VMEM((8, 32, 128), F32),
             pltpu.VMEM((4, 16, 128), F32),
             pltpu.VMEM((8, 16, 128), F32),
             pltpu.VMEM((8, 16, 128), F32),
             pltpu.SemaphoreType.DMA((5,)),
-            pltpu.SemaphoreType.DMA((38,)),
-            pltpu.SemaphoreType.DMA((38,)),
+            pltpu.SemaphoreType.DMA((73,)),
+            pltpu.SemaphoreType.DMA((73,)),
         ],
-        compiler_params=pltpu.CompilerParams(collective_id=0, has_side_effects=True, vmem_limit_bytes=40 * 2**20),
+        compiler_params=pltpu.CompilerParams(collective_id=0, has_side_effects=True, vmem_limit_bytes=62 * 2**20),
     )(table, signs.reshape(128, 128), samples.reshape(64, 128))
 
 

time: 54.5 us -> 51.1 us (0.938)
  Pallas kernels: 49.2 us -> 47.4 us
  local copies, waits for them, and re-layouts: 4.42 us -> 2.8 us
    pallas_call x1, Pallas kernels: 49.2 us -> 47.4 us  [per_device(): pl.pallas_call(kernel, out_shape=(jax.ShapeDtypeStruct((32, 128), F32), j...]
    unnamed x8 -> x2, local copies, waits for them, and re-layouts: 4.42 us -> 2.8 us
where the time goes in v3:
time: 51.1 us; the launch traced here: 50.9 us
  Pallas kernels  47.4 us (93%)
  local copies, waits for them, and re-layouts  2.8 us (5%)
  between operations  0.64 us (1%)
    pallas_call x1, Pallas kernels, per_device(): pl.pallas_call(kernel, out_shape=(jax.ShapeDtypeStruct((32, 128), F32), j...  47.4 us
    unnamed x2, local copies, waits for them, and re-layouts  2.8 us

profile of v3, /device:TPU:1, one launch (start us, length us, event | category | flops | bytes accessed | tf_op | source)
XLA Modules:
  0.0 50.9 jit_solution(10112909563902940255)
XLA Ops:
  0.6 47.4 %shard_map.50 = (f32[32,128]{1,0:T(8,128)}, f32[128,128]{1,0:T(8,128)}) custom-call(f32[32,16384]{1,0:T(8,128)} %table_hbm.1, s32[128,128]{1,0:T(8,128)} %bitcast.2, s32[64,128]{1,0:T(8,128)} %bitcast.3), custom_call_target="tpu_custom_call" | custom-call | tf_op jit(solution)/shard_map/pallas_call | solution.py:256
  48.1 1.3 %copy.7 = f32[32,128]{1,0:T(8,128)} copy(f32[32,128]{1,0:T(8,128)} %get-tuple-element.4) | data formatting | bytes 32768
  49.4 1.5 %copy.8 = f32[128,128]{1,0:T(8,128)} copy(f32[128,128]{1,0:T(8,128)} %get-tuple-element.5) | data formatting | bytes 131072

commit v4 on v3

--- a/solution.py
+++ b/solution.py
@@ -9,6 +9,7 @@
 BF16 = jnp.bfloat16
 MESH = pl.DeviceIdType.MESH
 NT = (((1,), (1,)), ((), ()))
+FIRST = 8
 
 
 def butterflies(parts):
@@ -36,7 +37,7 @@
 
 def kernel(
     table_hbm, signs_hbm, samples_hbm, sketch, gram,
-    table, signs, samples, xs, hi, lo, rows_of, index_v, index_s, sign_of, terms_z, z1, total_z, z2, terms, r1, total, r2,
+    table, signs, flips, samples, xs, hi, lo, rows_of, index_v, index_s, sign_of, terms_z, z1, total_z, z2, terms, r1, total, r2,
     whole, r3, r4, blocks,
     load, send, recv,
 ):
@@ -44,9 +45,6 @@
     col = lax.axis_index("col")
     y, z, x = row // 16, (row // 2) % 8, row % 2
     line_place = x * 4 + col
-
-    def plane(dy, dx):
-        return (y + dy) % 4, (x + dx) % 2
 
     def at(y, z, x):
         return {"row": y * 16 + z * 2 + x}
@@ -65,8 +63,8 @@
     for copy in copies_in:
         copy.start()
     barrier = pltpu.get_barrier_semaphore()
-    met = [at(*(lambda o: (o[0], z, o[1]))(plane(dy, dx))) for dy, dx in partners]
-    met += [at(y, (z + k) % 8, x) for k in range(1, 8)]
+    met = [at(y, (z + k) % 8, x) for k in (4, 3, 5, 2, 6, 1, 7)]
+    met += [at((y + dy) % 4, z, (x + dx) % 2) for dy, dx in partners]
     met += [{"row": y * 16 + z * 2 + (x + dx) % 2, "col": (col + dc) % 4} for dx in range(2) for dc in range(1, 4)]
     for device in met:
         pl.semaphore_signal(barrier, inc=1, device_id=device, device_id_type=MESH)
@@ -75,6 +73,7 @@
     j = lax.broadcasted_iota(jnp.int32, (256, 256), 1)
     walsh = ((1 - 2 * parity(i & j)).astype(F32) * F32(1 / 1024)).astype(BF16)
     copies_in[0].wait()
+    flips[...] = signs[...].astype(F32)
     for h in range(2):
         rows = slice(16 * h, 16 * h + 16)
         copies_in[1 + 2 * h].wait()
@@ -83,7 +82,7 @@
                 parts = []
                 for u in range(8):
                     c = u * 16 + w * 2 + t
-                    parts.append(table[rows, c * 128:(c + 1) * 128] * signs[c:c + 1, :].astype(F32))
+                    parts.append(table[rows, c * 128:(c + 1) * 128] * flips[c:c + 1, :])
                 for u, p in enumerate(butterflies(parts)):
                     c = u * 16 + w * 2 + t
                     xs[rows, c * 128:(c + 1) * 128] = p
@@ -97,23 +96,21 @@
                     lo[w, put, t * 128:(t + 1) * 128] = b
         if h == 0:
             copies_in[2].wait()
-            index_v[...] = samples[...] & 16383
+            local = samples[...] & 16383
+            group = lax.broadcasted_iota(jnp.int32, (64, 128), 1) >> 5
+            turn = (group - (local >> 11)) & 3
+            index_v[...] = turn * 4096 + (local >> 13) * 2048 + (local & 2047)
             index_copy = pltpu.make_async_copy(index_v, index_s, load.at[4])
             index_copy.start()
             sign_of[...] = (1 - 2 * parity((samples[...] >> 14) & row)).astype(F32)
-    lane = lax.broadcasted_iota(jnp.int32, (256, 128), 1)
-    below = [lane < 32, lane < 64, lane < 96]
     for w in range(8):
         done = lax.dot_general(walsh, hi[w], NT, preferred_element_type=F32)
         done = done + lax.dot_general(walsh, lo[w], NT, preferred_element_type=F32)
         for half in range(2):
             tile = done[:, half * 128:half * 128 + 128]
-            rolled = [tile] + [pltpu.roll(tile, 32 * k, 1) for k in (1, 2, 3)]
-            for v in range(4):
-                r = [rolled[(g - v) % 4] for g in range(4)]
-                four = jnp.where(below[0], r[0], jnp.where(below[1], r[1], jnp.where(below[2], r[2], r[3])))
-                u = half * 4 + v
-                rows_of[u * 2048 + w * 256:u * 2048 + w * 256 + 256, :] = four
+            for k in range(4):
+                put = k * 4096 + half * 2048 + w * 256
+                rows_of[put:put + 256, :] = pltpu.roll(tile, 32 * k, 1) if k else tile
     index_copy.wait()
     pl.semaphore_wait(barrier, len(met))
 
@@ -123,34 +120,33 @@
         (lax.broadcasted_iota(jnp.int32, (128, 128), 0) >> 5) == (lax.broadcasted_iota(jnp.int32, (128, 128), 1) >> 5)
     ).astype(BF16)
 
-    def own(first, count):
-        shape = (count, 128)
-        return (lax.broadcasted_iota(jnp.int32, shape, 1) & 31) == lax.broadcasted_iota(jnp.int32, shape, 0) + first
-
-    def gather(into, to, first, count, rs):
-        mask = own(first, count)
+    def gather(into, places, first, count, rs):
+        padded = -(-count // 8) * 8
+        mask = (lax.broadcasted_iota(jnp.int32, (padded, 128), 1) & 31) == (
+            lax.broadcasted_iota(jnp.int32, (padded, 128), 0) + first
+        )
         picked = [jnp.where(mask, sign_of[pl.ds(r, 1), :], F32(0)) for r in rs]
         factor = jnp.dot(jnp.concatenate(picked, axis=0).astype(BF16), spread, preferred_element_type=F32)
-        for n, r in enumerate(rs):
+        for place, r in zip(places, rs):
             for p in range(count):
                 v = [rows_of[pl.ds(index_s[r, g * 32 + first + p], 1), :] for g in range(4)]
                 four = jnp.where(below1[0], v[0], jnp.where(below1[1], v[1], jnp.where(below1[2], v[2], v[3])))
-                into[pl.ds(to + n * count + p, 1), :] = four
-        here = pl.ds(pl.multiple_of(to, 8), len(rs) * count)
-        into[here, :] = into[here, :] * factor
+                into[place + (pl.ds(p, 1), slice(None))] = four
+        for i, place in enumerate(places):
+            into[place] = into[place] * factor[i * padded:i * padded + count]
 
     def gather_z(n):
         _, other = line(n)
 
         def four(q, carry):
-            gather(terms_z, n * 64 + q * 32, 0, 8, [(2 * q + e // 2) * 16 + other * 2 + e % 2 for e in range(4)])
+            gather(terms_z, [(n, q * 4 + e) for e in range(4)], 0, FIRST, [(2 * q + e // 2) * 16 + other * 2 + e % 2 for e in range(4)])
             return carry
 
         lax.fori_loop(0, 2, four, 0)
 
     def gather_yx(n, s):
         y_of, x_of = turned(n)
-        gather(terms, n * 192 + s * 48, 8, 24, [y_of * 16 + (2 * s + j) * 2 + x_of for j in range(2)])
+        gather(terms, [(n, 2 * s + j) for j in range(2)], FIRST, 32 - FIRST, [y_of * 16 + (2 * s + j) * 2 + x_of for j in range(2)])
 
     def line(n):
         k = jnp.where(n == 7, 0, (n + 4) % 8 + n // 4)
@@ -170,11 +166,11 @@
         return copy
 
     def sent_z(n):
-        return remote(terms_z.at[pl.ds(n * 64, 64)], z1.at[n], n, at(y, line(n)[1], x))
+        return remote(terms_z.at[n], z1.at[n], n, at(y, line(n)[1], x))
 
     def sent_yx(n, s):
         y_of, x_of = turned(n)
-        return remote(terms.at[pl.ds(n * 192 + s * 48, 48)], r1.at[n, pl.ds(s * 48, 48)], 7 + n * 4 + s, at(y_of, z, x_of))
+        return remote(terms.at[n, pl.ds(2 * s, 2)], r1.at[n, pl.ds(2 * s, 2)], 7 + n * 4 + s, at(y_of, z, x_of))
 
     started = []
 
@@ -200,7 +196,7 @@
             sent_yx(n, s).start()
             return carry
 
-        lax.fori_loop(2 * s, jnp.minimum(2 * s + 2, 7), of_z, 0)
+        lax.fori_loop(jnp.where(s == 0, 0, jnp.minimum(2 * s + 1, 7)), jnp.minimum(2 * s + 3, 7), of_z, 0)
         lax.fori_loop(0, 7, of_yx, 0)
         return carry
 
@@ -213,21 +209,21 @@
 
     lax.fori_loop(0, 4, of_own, 0)
     landed([sent_z(n) for n in range(7)])
-    total_z[...] = added(terms_z[7 * 64:8 * 64, :], z1)
+    total_z[...] = added(terms_z[7], z1)
     copies_z = []
     for n in range(7):
         y_of, x_of = turned(n)
-        copies_z.append(start(total_z.at[pl.ds((y_of * 2 + x_of) * 8, 8)], z2.at[n], 35 + n, at(y_of, z, x_of)))
+        copies_z.append(start(total_z.at[y_of * 2 + x_of], z2.at[n], 35 + n, at(y_of, z, x_of)))
     landed([sent_yx(n, s) for s in range(4) for n in range(7)])
-    total[...] = added(terms[7 * 192:8 * 192, :], r1)
+    total[...] = added(terms[7], r1)
     copies = []
     for n in range(7):
         other = line(n)[1]
-        copies.append(start(total.at[pl.ds(other * 24, 24)], r2.at[n], 42 + n, at(y, other, x)))
+        copies.append(start(total.at[other], r2.at[n], 42 + n, at(y, other, x)))
     landed(copies_z)
-    acc_z = added(total_z[pl.ds(pl.multiple_of((y * 2 + x) * 8, 8), 8), :], z2)
+    acc_z = added(total_z[y * 2 + x], z2)
     landed(copies)
-    acc = jnp.concatenate([acc_z, added(total[pl.ds(pl.multiple_of(z * 24, 8), 24), :], r2)], axis=0)
+    acc = jnp.concatenate([acc_z, added(total[z], r2)], axis=0)
     mine = jnp.concatenate([acc[:, g * 32:g * 32 + 32].T for g in range(4)], axis=1)
     sketch[...] = mine
     whole[line_place] = mine
@@ -261,6 +257,7 @@
         scratch_shapes=[
             pltpu.VMEM((32, 16384), F32),
             pltpu.VMEM((128, 128), jnp.int32),
+            pltpu.VMEM((128, 128), F32),
             pltpu.VMEM((64, 128), jnp.int32),
             pltpu.VMEM((32, 16384), F32),
             pltpu.VMEM((8, 256, 256), BF16),
@@ -269,14 +266,14 @@
             pltpu.VMEM((64, 128), jnp.int32),
             pltpu.SMEM((64, 128), jnp.int32),
             pltpu.VMEM((64, 128), F32),
-            pltpu.VMEM((512, 128), F32),
-            pltpu.VMEM((7, 64, 128), F32),
-            pltpu.VMEM((64, 128), F32),
-            pltpu.VMEM((7, 8, 128), F32),
-            pltpu.VMEM((1536, 128), F32),
-            pltpu.VMEM((7, 192, 128), F32),
-            pltpu.VMEM((192, 128), F32),
-            pltpu.VMEM((7, 24, 128), F32),
+            pltpu.VMEM((8, 8, FIRST, 128), F32),
+            pltpu.VMEM((7, 8, FIRST, 128), F32),
+            pltpu.VMEM((8, FIRST, 128), F32),
+            pltpu.VMEM((7, FIRST, 128), F32),
+            pltpu.VMEM((8, 8, 32 - FIRST, 128), F32),
+            pltpu.VMEM((7, 8, 32 - FIRST, 128), F32),
+            pltpu.VMEM((8, 32 - FIRST, 128), F32),
+            pltpu.VMEM((7, 32 - FIRST, 128), F32),
             pltpu.VMEM((8, 32, 128), F32),
             pltpu.VMEM((4, 16, 128), F32),
             pltpu.VMEM((8, 16, 128), F32),
@@ -285,7 +282,7 @@
             pltpu.SemaphoreType.DMA((73,)),
             pltpu.SemaphoreType.DMA((73,)),
         ],
-        compiler_params=pltpu.CompilerParams(collective_id=0, has_side_effects=True, vmem_limit_bytes=62 * 2**20),
+        compiler_params=pltpu.CompilerParams(collective_id=0, has_side_effects=True, vmem_limit_bytes=55104 * 2**10),
     )(table, signs.reshape(128, 128), samples.reshape(64, 128))
 
 

time: 51.1 us -> 48.9 us (0.957)
  Pallas kernels: 47.4 us -> 46.1 us
  local copies, waits for them, and re-layouts: 2.8 us -> 1.99 us
    pallas_call x1, Pallas kernels: 47.4 us -> 46.1 us  [per_device(): pl.pallas_call(kernel, out_shape=(jax.ShapeDtypeStruct((32, 128), F32), j...]
    unnamed x2 -> x4, local copies, waits for them, and re-layouts: 2.8 us -> 1.99 us
where the time goes in v4:
time: 48.9 us; the launch traced here: 48.7 us
  Pallas kernels  46.1 us (94%)
  local copies, waits for them, and re-layouts  1.99 us (4%)
  between operations  0.65 us (1%)
    pallas_call x1, Pallas kernels, per_device(): pl.pallas_call(kernel, out_shape=(jax.ShapeDtypeStruct((32, 128), F32), j...  46.1 us
    unnamed x4, local copies, waits for them, and re-layouts  1.99 us

profile of v4, /device:TPU:1, one launch (start us, length us, event | category | flops | bytes accessed | tf_op | source)
XLA Modules:
  0.0 48.7 jit_solution(8062015670151608387)
XLA Ops:
  0.6 0.0 copy-start
  0.6 0.7 %copy-done = s32[8192]{0:T(1024)S(1)} copy-done((s32[8192]{0:T(1024)S(1)}, s32[8192]{0:T(1024)}, u32[]{:S(2)}) %copy-start) | copy-done | bytes 32792
  1.4 46.1 %shard_map.50 = (f32[32,128]{1,0:T(8,128)S(1)}, f32[128,128]{1,0:T(8,128)S(1)}) custom-call(f32[32,16384]{1,0:T(8,128)} %table_hbm.1, s32[128,128]{1,0:T(8,128)} %bitcast.3, s32[64,128]{1,0:T(8,128)S(1)} %bitcast.2), custom_call_target="tpu_custom_call" | custom-call | tf_op jit(solution)/shard_map/pallas_call | solution.py:252
  47.5 0.6 %copy.7 = f32[32,128]{1,0:T(8,128)} copy(f32[32,128]{1,0:T(8,128)S(1)} %get-tuple-element.4) | data formatting | bytes 32768
  48.1 0.6 %copy.8 = f32[128,128]{1,0:T(8,128)} copy(f32[128,128]{1,0:T(8,128)S(1)} %get-tuple-element.5) | data formatting | bytes 131072
Async XLA Ops:
  0.6 0.8 %copy-start = (s32[8192]{0:T(1024)S(1)}, s32[8192]{0:T(1024)}, u32[]{:S(2)}) copy-start(s32[8192]{0:T(1024)} %param.5) | copy-start | bytes 98308

commit v5 on v4

--- a/solution.py
+++ b/solution.py
@@ -56,9 +56,11 @@
     partners = [(2, 1), (1, 1), (3, 1), (2, 0), (0, 1), (1, 0), (3, 0)]
     copies_in = [
         pltpu.make_async_copy(signs_hbm, signs, load.at[0]),
-        pltpu.make_async_copy(table_hbm.at[pl.ds(0, 16)], table.at[pl.ds(0, 16)], load.at[1]),
-        pltpu.make_async_copy(samples_hbm, samples, load.at[2]),
-        pltpu.make_async_copy(table_hbm.at[pl.ds(16, 16)], table.at[pl.ds(16, 16)], load.at[3]),
+        pltpu.make_async_copy(table_hbm.at[pl.ds(0, 8)], table.at[pl.ds(0, 8)], load.at[1]),
+        pltpu.make_async_copy(table_hbm.at[pl.ds(8, 8)], table.at[pl.ds(8, 8)], load.at[2]),
+        pltpu.make_async_copy(samples_hbm, samples, load.at[3]),
+        pltpu.make_async_copy(table_hbm.at[pl.ds(16, 8)], table.at[pl.ds(16, 8)], load.at[4]),
+        pltpu.make_async_copy(table_hbm.at[pl.ds(24, 8)], table.at[pl.ds(24, 8)], load.at[5]),
     ]
     for copy in copies_in:
         copy.start()
@@ -76,7 +78,8 @@
     flips[...] = signs[...].astype(F32)
     for h in range(2):
         rows = slice(16 * h, 16 * h + 16)
-        copies_in[1 + 2 * h].wait()
+        copies_in[1 + 3 * h].wait()
+        copies_in[2 + 3 * h].wait()
         for t in range(2):
             for w in range(8):
                 parts = []
@@ -95,12 +98,12 @@
                     hi[w, put, t * 128:(t + 1) * 128] = a
                     lo[w, put, t * 128:(t + 1) * 128] = b
         if h == 0:
-            copies_in[2].wait()
+            copies_in[3].wait()
             local = samples[...] & 16383
             group = lax.broadcasted_iota(jnp.int32, (64, 128), 1) >> 5
             turn = (group - (local >> 11)) & 3
             index_v[...] = turn * 4096 + (local >> 13) * 2048 + (local & 2047)
-            index_copy = pltpu.make_async_copy(index_v, index_s, load.at[4])
+            index_copy = pltpu.make_async_copy(index_v, index_s, load.at[6])
             index_copy.start()
             sign_of[...] = (1 - 2 * parity((samples[...] >> 14) & row)).astype(F32)
     for w in range(8):
@@ -175,6 +178,9 @@
     started = []
 
     def landed(copies):
+        for copy in started:
+            copy.wait_send()
+        started.clear()
         for copy in copies:
             copy.wait_recv()
         started.extend(copies)
@@ -228,11 +234,14 @@
     sketch[...] = mine
     whole[line_place] = mine
     landed([start(whole.at[line_place], whole.at[line_place], 49 + k - 1, x_line(k)) for k in range(1, 8)])
-    part = jnp.zeros((16, 128), F32)
-    for half in range(2):
-        every = jnp.concatenate([whole[half * 4 + c] for c in range(4)], axis=0)
-        left = whole[half * 4 + line_place // 2, pl.ds(pl.multiple_of((line_place % 2) * 16, 16), 16), :]
-        part = part + lax.dot_general(left, every, NT, precision=lax.Precision.HIGHEST, preferred_element_type=F32)
+    every = [split(jnp.concatenate([whole[half * 4 + c] for c in range(4)], axis=0)) for half in range(2)]
+    high, low = (jnp.concatenate([pieces[i] for pieces in every], axis=1) for i in range(2))
+    rows16 = pl.ds(pl.multiple_of((line_place % 2) * 16, 16), 16)
+    left = [split(whole[half * 4 + line_place // 2, rows16, :]) for half in range(2)]
+    left_high, left_low = (jnp.concatenate([pieces[i] for pieces in left], axis=1) for i in range(2))
+    part = lax.dot_general(left_high, high, NT, preferred_element_type=F32)
+    part = part + lax.dot_general(left_high, low, NT, preferred_element_type=F32)
+    part = part + lax.dot_general(left_low, high, NT, preferred_element_type=F32)
     r3[y] = part
     landed([start(r3.at[y], r3.at[y], 56 + k - 1, at((y + k) % 4, z, x)) for k in (2, 1, 3)])
     acc = (r3[0] + r3[1]) + (r3[2] + r3[3])
@@ -278,12 +287,12 @@
             pltpu.VMEM((4, 16, 128), F32),
             pltpu.VMEM((8, 16, 128), F32),
             pltpu.VMEM((8, 16, 128), F32),
-            pltpu.SemaphoreType.DMA((5,)),
+            pltpu.SemaphoreType.DMA((7,)),
             pltpu.SemaphoreType.DMA((73,)),
             pltpu.SemaphoreType.DMA((73,)),
         ],
-        compiler_params=pltpu.CompilerParams(collective_id=0, has_side_effects=True, vmem_limit_bytes=55104 * 2**10),
-    )(table, signs.reshape(128, 128), samples.reshape(64, 128))
+        compiler_params=pltpu.CompilerParams(collective_id=0, has_side_effects=True, vmem_limit_bytes=40 * 2**20),
+    )(*(pltpu.with_memory_space_constraint(a, pltpu.HBM) for a in (table, signs.reshape(128, 128), samples.reshape(64, 128))))
 
 
 def solution(mesh):

time: 48.9 us -> 48 us (0.982)
  local copies, waits for them, and re-layouts: 1.99 us -> 1.24 us
    unnamed x4 -> x2, local copies, waits for them, and re-layouts: 1.99 us -> 1.24 us
where the time goes in v5:
time: 48 us; the launch traced here: 47.9 us
  Pallas kernels  46 us (96%)
  local copies, waits for them, and re-layouts  1.24 us (3%)
  between operations  0.64 us (1%)
    pallas_call x1, Pallas kernels, per_device(): pl.pallas_call(kernel, out_shape=(jax.ShapeDtypeStruct((32, 128), F32), j...  46 us
    unnamed x2, local copies, waits for them, and re-layouts  1.24 us

profile of v5, /device:TPU:1, one launch (start us, length us, event | category | flops | bytes accessed | tf_op | source)
XLA Modules:
  0.0 47.9 jit_solution(3405239770519195336)
XLA Ops:
  0.6 46.0 %shard_map.50 = (f32[32,128]{1,0:T(8,128)S(1)}, f32[128,128]{1,0:T(8,128)S(1)}) custom-call(f32[32,16384]{1,0:T(8,128)} %table_hbm.1, s32[128,128]{1,0:T(8,128)} %bitcast.2, s32[64,128]{1,0:T(8,128)} %bitcast.3), custom_call_target="tpu_custom_call" | custom-call | tf_op jit(solution)/shard_map/pallas_call | solution.py:261
  46.6 0.6 %copy.7 = f32[32,128]{1,0:T(8,128)} copy(f32[32,128]{1,0:T(8,128)S(1)} %get-tuple-element.4) | data formatting | bytes 32768
  47.2 0.6 %copy.8 = f32[128,128]{1,0:T(8,128)} copy(f32[128,128]{1,0:T(8,128)S(1)} %get-tuple-element.5) | data formatting | bytes 131072

commit v6 on v5

--- a/solution.py
+++ b/solution.py
@@ -255,12 +255,20 @@
         copy.wait_send()
 
 
+def copy_kernel(a_in, b_in, a_out, b_out, sem):
+    copies = [pltpu.make_async_copy(a_in, a_out, sem.at[0]), pltpu.make_async_copy(b_in, b_out, sem.at[1])]
+    for copy in copies:
+        copy.start()
+    for copy in copies:
+        copy.wait()
+
+
 def per_device(table, signs, samples):
     hbm = pl.BlockSpec(memory_space=pltpu.HBM)
     vmem = pl.BlockSpec(memory_space=pltpu.VMEM)
-    return pl.pallas_call(
+    results = pl.pallas_call(
         kernel,
-        out_shape=(jax.ShapeDtypeStruct((32, 128), F32), jax.ShapeDtypeStruct((128, 128), F32)),
+        out_shape=(pltpu.VMEM((32, 128), F32), pltpu.VMEM((128, 128), F32)),
         in_specs=[hbm] * 3,
         out_specs=(vmem, vmem),
         scratch_shapes=[
@@ -293,6 +301,15 @@
         ],
         compiler_params=pltpu.CompilerParams(collective_id=0, has_side_effects=True, vmem_limit_bytes=40 * 2**20),
     )(*(pltpu.with_memory_space_constraint(a, pltpu.HBM) for a in (table, signs.reshape(128, 128), samples.reshape(64, 128))))
+    held = pl.BlockSpec(memory_space=pltpu.VMEM)
+    return pl.pallas_call(
+        copy_kernel,
+        out_shape=(jax.ShapeDtypeStruct((32, 128), F32), jax.ShapeDtypeStruct((128, 128), F32)),
+        in_specs=[held] * 2,
+        out_specs=(hbm, hbm),
+        scratch_shapes=[pltpu.SemaphoreType.DMA((2,))],
+        compiler_params=pltpu.CompilerParams(vmem_limit_bytes=16 * 2**20),
+    )(*results)
 
 
 def solution(mesh):

time: 48 us -> 47.4 us (0.987)
  local copies, waits for them, and re-layouts: 1.24 us -> 0 us
  Pallas kernels: 46 us -> 46.7 us
    unnamed x2 -> x0, local copies, waits for them, and re-layouts: 1.24 us -> none
    pallas_call x1 -> x2, Pallas kernels: 46 us -> 46.7 us  [the longest x1 46 us: per_device(): pl.pallas_call(kernel, out_shape=(pltpu.VMEM((32, 128), F32), pltpu.VMEM(...]
where the time goes in v6:
time: 47.4 us; the launch traced here: 47.3 us
  Pallas kernels  46.7 us (99%)
  between operations  0.64 us (1%)
    pallas_call x1, Pallas kernels, per_device(): pl.pallas_call(kernel, out_shape=(pltpu.VMEM((32, 128), F32), pltpu.VMEM(...  46 us

profile of v6, /device:TPU:1, one launch (start us, length us, event | category | flops | bytes accessed | tf_op | source)
XLA Modules:
  0.0 47.3 jit_solution(9442767172811682924)
XLA Ops:
  0.6 46.0 %shard_map.50 = (f32[32,128]{1,0:T(8,128)S(1)}, f32[128,128]{1,0:T(8,128)S(1)}) custom-call(f32[32,16384]{1,0:T(8,128)} %table_hbm.1, s32[128,128]{1,0:T(8,128)} %bitcast.2, s32[64,128]{1,0:T(8,128)} %bitcast.3), custom_call_target="tpu_custom_call" | custom-call | tf_op jit(solution)/shard_map/pallas_call | solution.py:269
  46.6 0.7 %shard_map.51 = (f32[32,128]{1,0:T(8,128)}, f32[128,128]{1,0:T(8,128)}) custom-call(f32[32,128]{1,0:T(8,128)S(1)} %get-tuple-element.4.a_in, f32[128,128]{1,0:T(8,128)S(1)} %get-tuple-element.5.b_in), custom_call_target="tpu_custom_call" | custom-call | tf_op jit(solution)/shard_map/pallas_call | solution.py:305

commit v7 on v6

--- a/solution.py
+++ b/solution.py
@@ -232,13 +232,10 @@
     acc = jnp.concatenate([acc_z, added(total[z], r2)], axis=0)
     mine = jnp.concatenate([acc[:, g * 32:g * 32 + 32].T for g in range(4)], axis=1)
     sketch[...] = mine
-    whole[line_place] = mine
-    landed([start(whole.at[line_place], whole.at[line_place], 49 + k - 1, x_line(k)) for k in range(1, 8)])
-    every = [split(jnp.concatenate([whole[half * 4 + c] for c in range(4)], axis=0)) for half in range(2)]
-    high, low = (jnp.concatenate([pieces[i] for pieces in every], axis=1) for i in range(2))
-    rows16 = pl.ds(pl.multiple_of((line_place % 2) * 16, 16), 16)
-    left = [split(whole[half * 4 + line_place // 2, rows16, :]) for half in range(2)]
-    left_high, left_low = (jnp.concatenate([pieces[i] for pieces in left], axis=1) for i in range(2))
+    whole[col] = mine
+    landed([start(whole.at[col], whole.at[col], 49 + k - 1, {"col": (col + k) % 4}) for k in range(1, 4)])
+    high, low = split(whole[0:4].reshape(128, 128))
+    left_high, left_low = split(mine)
     part = lax.dot_general(left_high, high, NT, preferred_element_type=F32)
     part = part + lax.dot_general(left_high, low, NT, preferred_element_type=F32)
     part = part + lax.dot_general(left_low, high, NT, preferred_element_type=F32)
@@ -250,7 +247,7 @@
     acc = ((r4[0] + r4[1]) + (r4[2] + r4[3])) + ((r4[4] + r4[5]) + (r4[6] + r4[7]))
     blocks[line_place] = acc * F32(1 / 8192)
     landed([start(blocks.at[line_place], blocks.at[line_place], 66 + k - 1, x_line(k)) for k in range(1, 8)])
-    gram[...] = blocks[...].reshape(128, 128)
+    gram[...] = (blocks[0:4] + blocks[4:8]).reshape(128, 128)
     for copy in started:
         copy.wait_send()
 
@@ -292,9 +289,9 @@
             pltpu.VMEM((8, 32 - FIRST, 128), F32),
             pltpu.VMEM((7, 32 - FIRST, 128), F32),
             pltpu.VMEM((8, 32, 128), F32),
-            pltpu.VMEM((4, 16, 128), F32),
-            pltpu.VMEM((8, 16, 128), F32),
-            pltpu.VMEM((8, 16, 128), F32),
+            pltpu.VMEM((4, 32, 128), F32),
+            pltpu.VMEM((8, 32, 128), F32),
+            pltpu.VMEM((8, 32, 128), F32),
             pltpu.SemaphoreType.DMA((7,)),
             pltpu.SemaphoreType.DMA((73,)),
             pltpu.SemaphoreType.DMA((73,)),

time: 47.4 us -> 47 us (level)
  Pallas kernels: 46.7 us -> 46.2 us
where the time goes in v7:
time: 47 us; the launch traced here: 46.9 us
  Pallas kernels  46.2 us (98%)
  between operations  0.64 us (1%)
    pallas_call x1, Pallas kernels, per_device(): pl.pallas_call(kernel, out_shape=(pltpu.VMEM((32, 128), F32), pltpu.VMEM(...  45.6 us

profile of v7, /device:TPU:1, one launch (start us, length us, event | category | flops | bytes accessed | tf_op | source)
XLA Modules:
  0.0 46.9 jit_solution(3408546614536689058)
XLA Ops:
  0.6 45.6 %shard_map.50 = (f32[32,128]{1,0:T(8,128)S(1)}, f32[128,128]{1,0:T(8,128)S(1)}) custom-call(f32[32,16384]{1,0:T(8,128)} %table_hbm.1, s32[128,128]{1,0:T(8,128)} %bitcast.2, s32[64,128]{1,0:T(8,128)} %bitcast.3), custom_call_target="tpu_custom_call" | custom-call | tf_op jit(solution)/shard_map/pallas_call | solution.py:266
  46.2 0.7 %shard_map.51 = (f32[32,128]{1,0:T(8,128)}, f32[128,128]{1,0:T(8,128)}) custom-call(f32[32,128]{1,0:T(8,128)S(1)} %get-tuple-element.4.a_in, f32[128,128]{1,0:T(8,128)S(1)} %get-tuple-element.5.b_in), custom_call_target="tpu_custom_call" | custom-call | tf_op jit(solution)/shard_map/pallas_call | solution.py:302

commit v8 on v7

--- a/solution.py
+++ b/solution.py
@@ -239,15 +239,16 @@
     part = lax.dot_general(left_high, high, NT, preferred_element_type=F32)
     part = part + lax.dot_general(left_high, low, NT, preferred_element_type=F32)
     part = part + lax.dot_general(left_low, high, NT, preferred_element_type=F32)
-    r3[y] = part
-    landed([start(r3.at[y], r3.at[y], 56 + k - 1, at((y + k) % 4, z, x)) for k in (2, 1, 3)])
-    acc = (r3[0] + r3[1]) + (r3[2] + r3[3])
+    place = y * 2 + x
+    r3[place] = part
+    landed([start(r3.at[place], r3.at[place], 52 + n, (lambda o: at(o[0], z, o[1]))(turned(n))) for n in range(7)])
+    acc = ((r3[0] + r3[1]) + (r3[2] + r3[3])) + ((r3[4] + r3[5]) + (r3[6] + r3[7]))
     r4[z] = acc
     landed([start(r4.at[z], r4.at[z], 59 + k - 1, at(y, (z + k) % 8, x)) for k in (4, 3, 5, 2, 6, 1, 7)])
     acc = ((r4[0] + r4[1]) + (r4[2] + r4[3])) + ((r4[4] + r4[5]) + (r4[6] + r4[7]))
-    blocks[line_place] = acc * F32(1 / 8192)
-    landed([start(blocks.at[line_place], blocks.at[line_place], 66 + k - 1, x_line(k)) for k in range(1, 8)])
-    gram[...] = (blocks[0:4] + blocks[4:8]).reshape(128, 128)
+    blocks[col] = acc * F32(1 / 8192)
+    landed([start(blocks.at[col], blocks.at[col], 66 + k - 1, {"col": (col + k) % 4}) for k in range(1, 4)])
+    gram[...] = blocks[0:4].reshape(128, 128)
     for copy in started:
         copy.wait_send()
 
@@ -289,7 +290,7 @@
             pltpu.VMEM((8, 32 - FIRST, 128), F32),
             pltpu.VMEM((7, 32 - FIRST, 128), F32),
             pltpu.VMEM((8, 32, 128), F32),
-            pltpu.VMEM((4, 32, 128), F32),
+            pltpu.VMEM((8, 32, 128), F32),
             pltpu.VMEM((8, 32, 128), F32),
             pltpu.VMEM((8, 32, 128), F32),
             pltpu.SemaphoreType.DMA((7,)),

time: 47 us -> 47 us (level)
  no operation moved by 1% of the time
where the time goes in v8:
time: 47 us; the launch traced here: 46.9 us
  Pallas kernels  46.3 us (99%)
  between operations  0.64 us (1%)
    pallas_call x1, Pallas kernels, per_device(): pl.pallas_call(kernel, out_shape=(pltpu.VMEM((32, 128), F32), pltpu.VMEM(...  45.6 us

profile of v8, /device:TPU:1, one launch (start us, length us, event | category | flops | bytes accessed | tf_op | source)
XLA Modules:
  0.0 46.9 jit_solution(7765284365722675367)
XLA Ops:
  0.6 45.6 %shard_map.50 = (f32[32,128]{1,0:T(8,128)S(1)}, f32[128,128]{1,0:T(8,128)S(1)}) custom-call(f32[32,16384]{1,0:T(8,128)} %table_hbm.1, s32[128,128]{1,0:T(8,128)} %bitcast.2, s32[64,128]{1,0:T(8,128)} %bitcast.3), custom_call_target="tpu_custom_call" | custom-call | tf_op jit(solution)/shard_map/pallas_call | solution.py:267
  46.3 0.7 %shard_map.51 = (f32[32,128]{1,0:T(8,128)}, f32[128,128]{1,0:T(8,128)}) custom-call(f32[32,128]{1,0:T(8,128)S(1)} %get-tuple-element.4.a_in, f32[128,128]{1,0:T(8,128)S(1)} %get-tuple-element.5.b_in), custom_call_target="tpu_custom_call" | custom-call | tf_op jit(solution)/shard_map/pallas_call | solution.py:303

commit v9 on v7

--- a/solution.py
+++ b/solution.py
@@ -81,22 +81,14 @@
         copies_in[1 + 3 * h].wait()
         copies_in[2 + 3 * h].wait()
         for t in range(2):
-            for w in range(8):
+            for u in range(8):
                 parts = []
-                for u in range(8):
+                for w in range(8):
                     c = u * 16 + w * 2 + t
                     parts.append(table[rows, c * 128:(c + 1) * 128] * flips[c:c + 1, :])
-                for u, p in enumerate(butterflies(parts)):
+                for w, p in enumerate(butterflies(parts)):
                     c = u * 16 + w * 2 + t
                     xs[rows, c * 128:(c + 1) * 128] = p
-            for u in range(8):
-                cs = [u * 16 + w * 2 + t for w in range(8)]
-                parts = [xs[rows, c * 128:(c + 1) * 128] for c in cs]
-                for w, p in enumerate(butterflies(parts)):
-                    a, b = split(p)
-                    put = slice(u * 32 + 16 * h, u * 32 + 16 * h + 16)
-                    hi[w, put, t * 128:(t + 1) * 128] = a
-                    lo[w, put, t * 128:(t + 1) * 128] = b
         if h == 0:
             copies_in[3].wait()
             local = samples[...] & 16383
@@ -106,7 +98,21 @@
             index_copy = pltpu.make_async_copy(index_v, index_s, load.at[6])
             index_copy.start()
             sign_of[...] = (1 - 2 * parity((samples[...] >> 14) & row)).astype(F32)
+    def split_part(w):
+        for h in range(2):
+            rows = slice(16 * h, 16 * h + 16)
+            for t in range(2):
+                cs = [u * 16 + w * 2 + t for u in range(8)]
+                for u, p in enumerate(butterflies([xs[rows, c * 128:(c + 1) * 128] for c in cs])):
+                    a, b = split(p)
+                    put = slice(u * 32 + 16 * h, u * 32 + 16 * h + 16)
+                    hi[w, put, t * 128:(t + 1) * 128] = a
+                    lo[w, put, t * 128:(t + 1) * 128] = b
+
+    split_part(0)
     for w in range(8):
+        if w < 7:
+            split_part(w + 1)
         done = lax.dot_general(walsh, hi[w], NT, preferred_element_type=F32)
         done = done + lax.dot_general(walsh, lo[w], NT, preferred_element_type=F32)
         for half in range(2):

time: 47 us -> 46.9 us (level)
  no operation moved by 1% of the time
where the time goes in v9:
time: 46.9 us
  Pallas kernels  46.2 us (99%)
  between operations  0.64 us (1%)
    pallas_call x1, Pallas kernels, per_device(): pl.pallas_call(kernel, out_shape=(pltpu.VMEM((32, 128), F32), pltpu.VMEM(...  45.6 us

profile of v9, /device:TPU:1, one launch (start us, length us, event | category | flops | bytes accessed | tf_op | source)
XLA Modules:
  0.0 46.9 jit_solution(10937588424213997997)
XLA Ops:
  0.6 45.6 %shard_map.50 = (f32[32,128]{1,0:T(8,128)S(1)}, f32[128,128]{1,0:T(8,128)S(1)}) custom-call(f32[32,16384]{1,0:T(8,128)} %table_hbm.1, s32[128,128]{1,0:T(8,128)} %bitcast.2, s32[64,128]{1,0:T(8,128)} %bitcast.3), custom_call_target="tpu_custom_call" | custom-call | tf_op jit(solution)/shard_map/pallas_call | solution.py:272
  46.2 0.7 %shard_map.51 = (f32[32,128]{1,0:T(8,128)}, f32[128,128]{1,0:T(8,128)}) custom-call(f32[32,128]{1,0:T(8,128)S(1)} %get-tuple-element.4.a_in, f32[128,128]{1,0:T(8,128)S(1)} %get-tuple-element.5.b_in), custom_call_target="tpu_custom_call" | custom-call | tf_op jit(solution)/shard_map/pallas_call | solution.py:308
